TPU v7x, 32 devices: a whole 2x2x4 slice. The times are simulated.
32 devices in a mesh: wave: 32 (over z, y, x, core), lev: 1.
Axes of the slice: x: 2, y: 2, z: 4, core: 2. Of those that a mesh axis runs over, the one named last changes fastest.
Arguments:
- spectra: bfloat16 [640, 16, 2, 640], P('wave', 'lev'), may hold values from -0.3125 to 0.3125
- legendre: bfloat16 [640, 32, 640], P('wave'), may hold values from -0.25 to 0.25
- wave_slots: int32 [640], replicated, may hold values from 0 to 639, each once
- row_cycle: int32 [32], replicated, may hold values from 0 to 1279, as said below
Outputs:
- grid_fields: bfloat16 [16, 32, 6144], P(None, 'wave', 'lev')
Inputs may be any that keep to these rules, and one draw needn't show every extreme that they name: `wave_slots`: each wavenumber 0 to 639 stands in exactly one slot; slot r lies on wave index r // 20. `row_cycle`: cycle numbers of distinct rows differ; cycle 0 and cycle 1280 - 1 both occur; row q lies on wave index q.
All inputs are finite; a program needn't handle non-finite values.
Results may differ from a plain program's by a relative error of at most 0.0055.
Values may be sent and summed in bfloat16 or wider, within the bound.
A program may use at most 64 MiB of HBM per device.

v0:
```python
from functools import partial
import math
import jax
import jax.numpy as jnp
from jax import lax
from jax.sharding import PartitionSpec as P

NLON = 6144
two_pi = 2.0 * math.pi


def twiddle_table(slot_waves, row_points, first_col, col_count):
    columns = first_col + lax.iota(jnp.int32, col_count)
    phase_int = slot_waves[:, None] * columns[None, :] % row_points
    angles = jnp.float32(two_pi) * phase_int.astype(jnp.float32) / row_points.astype(jnp.float32)
    weight = jnp.where(slot_waves == 0, jnp.float32(1.0), jnp.float32(2.0))[:, None]
    inside = (columns < row_points)[None, :]
    cosine = jnp.where(inside, weight * jnp.cos(angles), jnp.float32(0.0))
    sine_part = jnp.where(inside, -weight * jnp.sin(angles), jnp.float32(0.0))
    return jnp.concatenate([cosine, sine_part], axis=0).astype(jnp.bfloat16)


def row_product(coeffs, twiddle):
    return jnp.dot(coeffs, twiddle, preferred_element_type=jnp.float32).astype(jnp.bfloat16)


def shards(spectra, legendre, wave_slots, row_cycle):
    slots_dev, pairs_dev, two_parts, degrees = spectra.shape
    wave_count = lax.axis_size("wave")
    level_count = lax.axis_size("lev")
    total_slots = slots_dev * wave_count
    wave_pos = lax.axis_index("wave")
    level_pos = lax.axis_index("lev")
    own_waves = lax.dynamic_slice_in_dim(wave_slots, wave_pos * slots_dev, slots_dev)
    degree = lax.iota(jnp.int32, degrees)
    keep_mask = degree[None, :] < (total_slots - own_waves)[:, None]
    masked = jnp.where(keep_mask[:, None, None, :], spectra, jnp.zeros((), spectra.dtype))
    fourier = jnp.einsum(
        "rpik,rlk->plir", masked, legendre, preferred_element_type=jnp.float32
    ).astype(jnp.bfloat16)
    by_rows = lax.all_to_all(fourier, "wave", split_axis=1, concat_axis=3, tiled=True)
    rows_dev = by_rows.shape[1]
    flat_width = 2 * total_slots
    own_cycles = lax.dynamic_slice_in_dim(row_cycle, wave_pos * rows_dev, rows_dev)
    region = NLON // level_count
    first_col = level_pos * region
    actives = []
    row_pos = 0
    row_points = 20 + 4 * own_cycles[row_pos]
    active = first_col < row_points
    twiddle = twiddle_table(wave_slots, row_points, first_col, region)
    tables = [twiddle]
    actives.append(active)
    piece = lax.all_gather(by_rows, "lev", axis=0, tiled=True)
    row_pos = 0
    coeffs = piece[:, row_pos].reshape(piece.shape[0], flat_width)
    product = partial(row_product, coeffs, tables[row_pos])
    results = [product()]
    return jnp.stack(results, axis=1)


def solution(mesh):
    placed = (P("wave", "lev", None, None), P("wave", None, None), P(), P())
    return jax.shard_map(
        shards, mesh=mesh, in_specs=placed, out_specs=P(None, "wave", "lev"), check_vma=False
    )
```

profile of v0, /device:TPU:0, one launch (start us, length us, event | category | flops | bytes accessed | tf_op | source)
XLA Modules:
  0.0 236.1 jit_solution(6809609361605725039)
XLA Ops:
  0.0 0.0 copy-start
  0.0 0.8 dynamic-slice_subtract_fusion
  0.8 0.1 iota_compare_fusion
  0.9 1.9 broadcast_select_fusion
  2.8 0.0 copy-done
  2.8 0.4 fusion.17
  3.2 0.6 copy.12
  3.7 1.0 reshape.32
  4.7 7.3 %all-to-all-start = ((bf16[32,2,320]{2,1,0:T(2,128)(2,1)}), bf16[32,2,320]{2,1,0:T(2,128)(2,1)S(1)}, u32[]{:S(2)}, u32[]{:S(2)}) async-start(bf16[32,2,320]{2,1,0:T(2,128)(2,1)} %reshape.32), calls=%async_computation | async-start | bytes 98304 | tf_op jit(solution)/shard_map/all_to_all | solution.py:41
  12.0 1.3 dynamic_slice.7
  13.9 0.7 compare_select_fusion
  14.6 213.3 %select_convert_fusion.1 = (bf16[640,6144]{1,0:T(8,128)(2,1)}, bf16[640,6144]{1,0:T(8,128)(2,1)}) fusion(f32[640]{0:T(1024)S(1)} %get-tuple-element.7, f32[]{:T(128)S(6)} %convert_element_type.19, pred[]{:T(512)S(6)} %lt.49, s32[]{:T(128)S(6)} %select_n.34, s32[640]{0:T(1024)} %param.6, pred[6144]{0:T(1024)(128)(4,1)S(1)} %iota_compare_fusion.1, ...), kind=kLoop, calls=%fused_computation.9 | loop fusion | flops 66846720 | bytes 15742473 | tf_op jit(solution)/shard_map/convert
  227.9 0.0 all-to-all-done
  227.9 0.4 reshape.33
  228.3 0.1 copy.13
  228.4 0.3 reshape_squeeze.3
  228.8 7.4 %fusion.14 = bf16[16,1,6144]{2,0,1:T(8,128)(2,1)} fusion(bf16[16,1280]{1,0:T(8,128)(2,1)S(1)} %reshape_squeeze.3, bf16[640,6144]{1,0:T(8,128)(2,1)} %get-tuple-element.6, bf16[640,6144]{1,0:T(8,128)(2,1)} %get-tuple-element.5), kind=kOutput, calls=%fused_computation.16 | convolution fusion | flops 283213824 | bytes 15966208 | tf_op jit(solution)/shard_map/dot_general | solution.py:24
  (2 shorter events, 0.0 us)
Async XLA Ops:
  0.0 2.8 %copy-start = (bf16[20,32,640]{2,1,0:T(8,128)(2,1)S(1)}, bf16[20,32,640]{2,1,0:T(8,128)(2,1)}, u32[]{:S(2)}) copy-start(bf16[20,32,640]{2,1,0:T(8,128)(2,1)} %param.5) | copy-start | bytes 2457604
  4.7 223.2 %all-to-all-start = ((bf16[32,2,320]{2,1,0:T(2,128)(2,1)}), bf16[32,2,320]{2,1,0:T(2,128)(2,1)S(1)}, u32[]{:S(2)}, u32[]{:S(2)}) async-start(bf16[32,2,320]{2,1,0:T(2,128)(2,1)} %reshape.32), calls=%async_computation | async-start | bytes 98304 | tf_op jit(solution)/shard_map/all_to_all | solution.py:41
where the time goes:
time: 236 us
  other arithmetic  217 us (92%)
  matrix products  7.76 us (3%)
  starting transfers between devices  7.3 us (3%)
  local copies, waits for them, and re-layouts  3.6 us (2%)
    another operation x1, other arithmetic  213 us
    dot_general x1, matrix products, row_product(): jnp.dot(coeffs, twiddle, preferred_element_type=jnp.float32)  7.38 us
    all_to_all x1, starting transfers between devices, shards(): lax.all_to_all(fourier, 'wave', split_axis=1, concat_axis=3, tiled=True)  7.3 us
  transfers between devices with their start and end apart: 1, of which 0 were waited for; matrix products, arithmetic and copies ran while one was open for 91% of the time, Pallas kernels for 0%

commit v1 on v0

--- a/solution.py
+++ b/solution.py
@@ -38,7 +38,10 @@
     fourier = jnp.einsum(
         "rpik,rlk->plir", masked, legendre, preferred_element_type=jnp.float32
     ).astype(jnp.bfloat16)
-    by_rows = lax.all_to_all(fourier, "wave", split_axis=1, concat_axis=3, tiled=True)
+    by_rows = jnp.concatenate(
+        lax.all_to_all(jnp.stack(jnp.split(fourier, lax.axis_size("wave"), axis=1)), "wave", 0, 0),
+        axis=3,
+    )
     rows_dev = by_rows.shape[1]
     flat_width = 2 * total_slots
     own_cycles = lax.dynamic_slice_in_dim(row_cycle, wave_pos * rows_dev, rows_dev)

time: 236 us -> 297 us (1.26)
  local copies, waits for them, and re-layouts: 3.6 us -> 65 us
    split x0 -> x33, local copies, waits for them, and re-layouts: none -> 28.7 us  [shards(): jnp.split(fourier, lax.axis_size('wave'), axis=1)]
    unnamed x4 -> x37, local copies, waits for them, and re-layouts: 1.32 us -> 24.3 us
    another operation x0 -> x33, local copies, waits for them, and re-layouts: none -> 10.3 us  [shards(): jnp.stack(jnp.split(fourier, lax.axis_size('wave'), axis=1))]
  transfers between devices with their start and end apart: 1 -> 1, of which waited for: 0 -> 0; matrix products, arithmetic and copies ran while one was open for 91% -> 72% of each run, Pallas kernels for 0% -> 0%
where the time goes in v1:
time: 297 us; the launch traced here: 296 us
  other arithmetic  215 us (72%)
  local copies, waits for them, and re-layouts  65 us (22%)
  matrix products  7.76 us (3%)
  starting transfers between devices  7.3 us (2%)
    another operation x1, other arithmetic  213 us
    split x33, local copies, waits for them, and re-layouts, shards(): jnp.split(fourier, lax.axis_size('wave'), axis=1)  28.7 us
    unnamed x37, local copies, waits for them, and re-layouts  24.3 us
    another operation x33, local copies, waits for them, and re-layouts, shards(): jnp.stack(jnp.split(fourier, lax.axis_size('wave'), axis=1))  10.3 us
    dot_general x1, matrix products, row_product(): jnp.dot(coeffs, twiddle, preferred_element_type=jnp.float32)  7.38 us
    all_to_all x1, starting transfers between devices, shards(): lax.all_to_all(jnp.stack(jnp.split(fourier, lax.axis_size('wave'), axis=1...  7.3 us
  transfers between devices with their start and end apart: 1, of which 0 were waited for; matrix products, arithmetic and copies ran while one was open for 72% of the time, Pallas kernels for 0%

profile of v1, /device:TPU:0, one launch (start us, length us, event | category | flops | bytes accessed | tf_op | source)
XLA Modules:
  0.0 296.1 jit_solution(18302508579050607357)
XLA Ops:
  0.9 1.9 broadcast_select_fusion
  3.2 1.8 fusion.23
  5.0 1.7 fusion.22
  6.7 1.2 copy.1568
  8.0 1.2 copy.1567
  9.4 1.2 copy.1566
  10.7 1.2 copy.1565
  12.1 1.2 copy.1564
  13.4 1.2 copy.1563
  14.8 1.2 copy.1562
  16.7 1.2 copy.1561
  28.3 1.2 copy.1586
  29.6 1.8 copy.1585
  40.8 1.3 constant_dynamic-update-slice_fusion.30
  42.1 1.3 constant_dynamic-update-slice_fusion.29
  43.4 1.3 constant_dynamic-update-slice_fusion.28
  44.7 1.3 constant_dynamic-update-slice_fusion.27
  46.0 1.3 constant_dynamic-update-slice_fusion.26
  47.3 1.3 constant_dynamic-update-slice_fusion.25
  63.7 1.4 copy.1619
  66.1 7.3 %all-to-all-start = ((bf16[32,2,320]{2,1,0:T(2,128)(2,1)}), bf16[32,2,320]{2,1,0:T(2,128)(2,1)S(1)}, u32[]{:S(2)}, u32[]{:S(2)}) async-start(bf16[32,2,320]{2,1,0:T(2,128)(2,1)} %reshape.38), calls=%async_computation | async-start | bytes 98304 | tf_op jit(solution)/shard_map/all_to_all | solution.py:42
  73.4 1.2 dynamic_slice.7
  75.3 212.6 %select_convert_fusion.1 = (bf16[640,6144]{1,0:T(8,128)(2,1)}, bf16[640,6144]{1,0:T(8,128)(2,1)}) fusion(f32[640]{0:T(1024)S(1)} %get-tuple-element.39, f32[]{:T(128)S(6)} %convert_element_type.19, pred[]{:T(512)S(6)} %lt.49, s32[]{:T(128)S(6)} %select_n.34, s32[640]{0:T(1024)S(1)} %copy-done.1, pred[6144]{0:T(1024)(128)(4,1)S(1)} %iota_compare_fusion.1, ...), kind=kLoop, calls=%fused_computation.9 | loop fusion | flops 66846720 | bytes 15742473 | tf_op jit(solution)/shard_map/convert
  288.8 7.4 %fusion.14 = bf16[16,1,6144]{2,0,1:T(8,128)(2,1)} fusion(bf16[16,1280]{1,0:T(8,128)(2,1)S(1)} %reshape_squeeze.3, bf16[640,6144]{1,0:T(8,128)(2,1)} %get-tuple-element.38, bf16[640,6144]{1,0:T(8,128)(2,1)} %get-tuple-element.37), kind=kOutput, calls=%fused_computation.16 | convolution fusion | flops 283213824 | bytes 15966208 | tf_op jit(solution)/shard_map/dot_general | solution.py:24
  (93 shorter events, 39.3 us)
Async XLA Ops:
  0.0 2.8 copy-start
  5.0 70.2 %copy-start.1 = (s32[640]{0:T(1024)S(1)}, s32[640]{0:T(1024)}, u32[]{:S(2)}) copy-start(s32[640]{0:T(1024)} %param.6) | copy-start | bytes 7684
  66.1 221.8 %all-to-all-start = ((bf16[32,2,320]{2,1,0:T(2,128)(2,1)}), bf16[32,2,320]{2,1,0:T(2,128)(2,1)S(1)}, u32[]{:S(2)}, u32[]{:S(2)}) async-start(bf16[32,2,320]{2,1,0:T(2,128)(2,1)} %reshape.38), calls=%async_computation | async-start | bytes 98304 | tf_op jit(solution)/shard_map/all_to_all | solution.py:42
